TPU v7x, 32 devices: a whole 2x2x4 slice. The times are simulated.
32 devices in a mesh: batch: 8 (over y, x, core), head: 4 (over z).
Axes of the slice: x: 2, y: 2, z: 4, core: 2. Of those that a mesh axis runs over, the one named last changes fastest.
Arguments:
- stream: bfloat16 [32768, 512], P(('batch', 'head')), may hold values from -3 to 3
- accumulator: float32 [32768, 512], P(('batch', 'head')), may hold values from -3 to 3
- inward: bfloat16 [3, 512, 512], P(None, None, 'head'), may hold values from -0.375 to 0.375
- inward_bias: bfloat16 [2, 512], P(None, 'head'), may hold values from -2.5 to 2.5
- outward: bfloat16 [512, 512], replicated, may hold values from -0.75 to 0.75
- outward_bias: float32 [512], replicated, may hold values from -2.5 to 2.5
- first_gain: float32 [512], replicated, may hold values from 0.25 to 1.75
- first_shift: float32 [512], replicated, may hold values from -2.5 to 2.5
- up_weight: bfloat16 [512, 2048], replicated, may hold values from -0.25 to 0.25
- up_bias: float32 [2048], replicated, may hold values from -2.5 to 2.5
- down_weight: bfloat16 [2048, 512], replicated, may hold values from -0.125 to 0.125
- down_bias: float32 [512], replicated, may hold values from -2.5 to 2.5
- second_gain: float32 [512], replicated, may hold values from 0.25 to 1.75
- second_shift: float32 [512], replicated, may hold values from -2.5 to 2.5
- long_count: int32 [8], P('batch'), may hold values from 0 to 4, as said below
- stream_cotangent: float32 [32768, 512], P(('batch', 'head')), may hold values from -3 to 3
- accumulator_cotangent: float32 [32768, 512], P(('batch', 'head')), may hold values from -3 to 3
Outputs:
- next_stream: bfloat16 [32768, 512], P(('batch', 'head'))
- next_accumulator: float32 [32768, 512], P(('batch', 'head'))
- stream_gradient: float32 [32768, 512], P(('batch', 'head'))
- inward_gradient: float32 [3, 512, 512], P(None, None, 'head')
- inward_bias_gradient: float32 [2, 512], P(None, 'head')
- outward_gradient: float32 [512, 512], replicated
- outward_bias_gradient: float32 [512], replicated
- first_gain_gradient: float32 [512], replicated
- first_shift_gradient: float32 [512], replicated
- up_weight_gradient: float32 [512, 2048], replicated
- up_bias_gradient: float32 [2048], replicated
- down_weight_gradient: float32 [2048, 512], replicated
- down_bias_gradient: float32 [512], replicated
- second_gain_gradient: float32 [512], replicated
- second_shift_gradient: float32 [512], replicated
Inputs may be any that keep to these rules, and one draw needn't show every extreme that they name: `long_count`: long sequences of 1024 tokens come first in their group, then sequences of 256 tokens fill it. Some group holds only long sequences and some holds none.
All inputs are finite; a program needn't handle non-finite values.
Results may differ from a plain program's by a relative error of at most 0.015.
Values may be sent and summed in bfloat16 or wider, within the bound.
No kernel may reach another device: no remote copies, remote signals or barrier semaphores. Data moves between devices by JAX's collectives and lax.ppermute only.
A program may use at most 128 MiB of HBM per device.

v0:
```python
import math

import jax
import jax.numpy as jnp
from jax import lax
from jax.sharding import PartitionSpec as P

HEAD_DIM = 64
LONG = 1024
SHORT = 256


WIDE_TYPE = jnp.float32
NARROW_TYPE = jnp.bfloat16


def layer_norm(hidden, norm_gain, norm_shift):
    average = jnp.mean(hidden, -1, keepdims=True)
    centered = hidden - average
    variance = jnp.mean(centered * centered, -1, keepdims=True)
    return centered * lax.rsqrt(variance + 1e-05) * norm_gain + norm_shift


def smooth_act(values):
    return jax.nn.gelu(values, approximate=False)


def segment_keys(positions, limit_rows):
    return jnp.where(positions < limit_rows, -1 - positions // LONG, positions // SHORT)


def contract_rows(left, right):
    return lax.dot_general(left, right, (((0,), (0,)), ((), ())), preferred_element_type=WIDE_TYPE)


def block_scores(query_rows, key_rows, segment):
    scores = jnp.einsum("qhe,khe->hqk", query_rows, key_rows, preferred_element_type=WIDE_TYPE) * (
        1.0 / math.sqrt(HEAD_DIM)
    )
    allowed = segment[:, None] == segment[None, :]
    return jnp.where(allowed[None], scores, -1e30)


def attend_forward(operands):
    query_rows, key_rows, value_rows, segment = operands
    scores = block_scores(query_rows, key_rows, segment)
    highest = jnp.max(scores, -1, keepdims=True)
    exponent = jnp.exp(scores - highest)
    row_sums = jnp.sum(exponent, -1, keepdims=True)
    attend_low = (exponent / row_sums).astype(NARROW_TYPE)
    output = jnp.einsum("hqk,khe->qhe", attend_low, value_rows, preferred_element_type=WIDE_TYPE)
    return (output.astype(NARROW_TYPE), (highest + jnp.log(row_sums))[..., 0])


def attend_backward(operands):
    query_rows, key_rows, value_rows, segment, log_sums, output_grad = operands
    scores = block_scores(query_rows, key_rows, segment)
    attend_full = jnp.exp(scores - log_sums[..., None])
    attend_low = attend_full.astype(NARROW_TYPE)
    value_grad = jnp.einsum(
        "hqk,qhe->khe", attend_low, output_grad, preferred_element_type=WIDE_TYPE
    )
    weights_grad = jnp.einsum(
        "qhe,khe->hqk", output_grad, value_rows, preferred_element_type=WIDE_TYPE
    )
    centre = jnp.sum(weights_grad * attend_full, -1, keepdims=True)
    score_grad = (attend_full * (weights_grad - centre)).astype(NARROW_TYPE)
    factor = 1.0 / math.sqrt(HEAD_DIM)
    query_grad = (
        jnp.einsum("hqk,khe->qhe", score_grad, key_rows, preferred_element_type=WIDE_TYPE) * factor
    )
    key_grad = (
        jnp.einsum("hqk,qhe->khe", score_grad, query_rows, preferred_element_type=WIDE_TYPE)
        * factor
    )
    return jnp.stack([query_grad, key_grad, value_grad], 1).astype(NARROW_TYPE)


def local_project(rows, inward, inward_bias):
    zero_column = jnp.zeros_like(inward_bias[0])
    projected = jnp.einsum("td,cde->tce", rows, inward, preferred_element_type=WIDE_TYPE)
    projected = projected + jnp.stack([inward_bias[0], zero_column, inward_bias[1]]).astype(
        WIDE_TYPE
    )
    return projected.astype(NARROW_TYPE)


def local_inward_grads(rows, input_grads):
    inward_grad = jnp.einsum("td,tce->cde", rows, input_grads, preferred_element_type=WIDE_TYPE)
    bias_grad = jnp.stack(
        [
            jnp.sum(input_grads[:, 0].astype(WIDE_TYPE), 0),
            jnp.sum(input_grads[:, 2].astype(WIDE_TYPE), 0),
        ]
    )
    return (inward_grad, bias_grad)


def body(
    stream,
    accumulator,
    inward,
    inward_bias,
    outward,
    outward_bias,
    first_gain,
    first_shift,
    up_weight,
    up_bias,
    down_weight,
    down_bias,
    second_gain,
    second_shift,
    long_count,
    stream_cotangent,
    accumulator_cotangent,
):
    token_rows = stream.shape[0]
    width_here = inward.shape[2]
    group_rows = token_rows * lax.axis_size("head")
    blocks = group_rows // LONG
    heads_here = width_here // HEAD_DIM
    gathered, full_inward = (
        lax.all_gather(stream, "head", axis=0, tiled=True),
        lax.all_gather(inward, "head", axis=2, tiled=True),
    )
    head_inputs = local_project(gathered, inward, inward_bias)
    block_shape = (blocks, LONG, heads_here, HEAD_DIM)
    query_blocks = head_inputs[:, 0].reshape(block_shape)
    key_blocks = head_inputs[:, 1].reshape(block_shape)
    value_blocks = head_inputs[:, 2].reshape(block_shape)
    positions = jnp.arange(group_rows, dtype=jnp.int32)
    segment = segment_keys(positions, long_count[0] * LONG).reshape(blocks, LONG)
    head_output, log_sums = lax.map(
        attend_forward, (query_blocks, key_blocks, value_blocks, segment)
    )
    head_output = head_output.reshape(group_rows, width_here)
    token_heads = lax.all_to_all(head_output, "head", split_axis=0, concat_axis=1, tiled=True)
    attention = jnp.dot(token_heads, outward, preferred_element_type=WIDE_TYPE) + outward_bias
    first_norm, first_pull = jax.vjp(
        layer_norm, stream.astype(WIDE_TYPE) + attention, first_gain, first_shift
    )
    first_low = first_norm.astype(NARROW_TYPE)
    preactivation = jnp.dot(first_low, up_weight, preferred_element_type=WIDE_TYPE) + up_bias
    activation, smooth_pull = jax.vjp(smooth_act, preactivation)
    hidden = activation.astype(NARROW_TYPE)
    branch = jnp.dot(hidden, down_weight, preferred_element_type=WIDE_TYPE) + down_bias
    second_norm, second_pull = jax.vjp(layer_norm, first_norm + branch, second_gain, second_shift)
    next_stream = second_norm.astype(NARROW_TYPE)
    next_accumulator = accumulator + attention + branch
    second_grad, second_gain_grad, second_shift_grad = second_pull(stream_cotangent)
    branch_grad = (second_grad + accumulator_cotangent).astype(NARROW_TYPE)
    down_weight_grad = contract_rows(hidden, branch_grad)
    down_bias_grad = jnp.sum(branch_grad.astype(WIDE_TYPE), 0)
    hidden_grad = jnp.einsum(
        "td,fd->tf", branch_grad, down_weight, preferred_element_type=WIDE_TYPE
    )
    (pre_grad,) = smooth_pull(hidden_grad)
    pre_grad = pre_grad.astype(NARROW_TYPE)
    up_weight_grad = contract_rows(first_low, pre_grad)
    up_bias_grad = jnp.sum(pre_grad.astype(WIDE_TYPE), 0)
    first_incoming = (
        jnp.einsum("tf,df->td", pre_grad, up_weight, preferred_element_type=WIDE_TYPE) + second_grad
    )
    first_grad, first_gain_grad, first_shift_grad = first_pull(first_incoming)
    attention_grad = (first_grad + accumulator_cotangent).astype(NARROW_TYPE)
    outward_grad = contract_rows(token_heads, attention_grad)
    outward_bias_grad = jnp.sum(attention_grad.astype(WIDE_TYPE), 0)
    heads_grad = jnp.einsum(
        "td,ed->te", attention_grad, outward, preferred_element_type=WIDE_TYPE
    ).astype(NARROW_TYPE)
    head_grads = lax.all_to_all(
        heads_grad, "head", split_axis=1, concat_axis=0, tiled=True
    ).reshape(block_shape)
    input_grads = lax.map(
        attend_backward, (query_blocks, key_blocks, value_blocks, segment, log_sums, head_grads)
    )
    input_grads = input_grads.reshape(group_rows, 3, width_here)
    inward_grad, inward_bias_grad = local_inward_grads(gathered, input_grads)
    token_grads = lax.all_to_all(input_grads, "head", split_axis=0, concat_axis=2, tiled=True)
    attend_stream = jnp.einsum(
        "tce,cde->td", token_grads, full_inward, preferred_element_type=WIDE_TYPE
    )
    inward_grad, inward_bias_grad = (
        lax.psum(inward_grad.astype(jnp.bfloat16), "batch").astype(jnp.float32),
        lax.psum(inward_bias_grad.astype(jnp.bfloat16), "batch").astype(jnp.float32),
    )
    shared = lax.psum(
        (
            outward_grad,
            outward_bias_grad,
            first_gain_grad,
            first_shift_grad,
            up_weight_grad,
            up_bias_grad,
            down_weight_grad,
            down_bias_grad,
            second_gain_grad,
            second_shift_grad,
        ),
        ("batch", "head"),
    )
    stream_gradient = first_grad + attend_stream
    return (
        next_stream,
        next_accumulator,
        stream_gradient,
        inward_grad,
        inward_bias_grad,
        shared[0],
        shared[1],
        shared[2],
        shared[3],
        shared[4],
        shared[5],
        shared[6],
        shared[7],
        shared[8],
        shared[9],
    )


def solution(mesh):
    in_specs = (
        P(("batch", "head"), None),
        P(("batch", "head"), None),
        P(None, None, "head"),
        P(None, "head"),
        P(),
        P(),
        P(),
        P(),
        P(),
        P(),
        P(),
        P(),
        P(),
        P(),
        P("batch"),
        P(("batch", "head"), None),
        P(("batch", "head"), None),
    )
    out_specs = (
        P(("batch", "head"), None),
        P(("batch", "head"), None),
        P(("batch", "head"), None),
        P(None, None, "head"),
        P(None, "head"),
        P(),
        P(),
        P(),
        P(),
        P(),
        P(),
        P(),
        P(),
        P(),
        P(),
    )
    return jax.shard_map(body, mesh=mesh, in_specs=in_specs, out_specs=out_specs, check_vma=False)
```

profile of v0, /device:TPU:0, one launch (start us, length us, event | category | flops | bytes accessed | tf_op | source)
XLA Modules:
  0.0 696.2 jit_solution(8411396920452839312)
XLA Ops:
  9.5 83.6 %all-gather.3.cloned.1.call-done = bf16[4096,512]{1,0:T(8,128)(2,1)} async-done(((bf16[1024,512]{1,0:T(8,128)(2,1)}), bf16[4096,512]{1,0:T(8,128)(2,1)}) %all-gather.3.cloned.1.call-update) | async-done | bytes 4194320 | tf_op jit(solution)/shard_map/all_gather | solution.py:124
  99.2 5.0 reshape.290
  104.2 5.9 copy.90
  116.5 5.0 reshape.292
  121.5 5.9 copy.92
  127.4 39.8 %while.22 = (s32[]{:T(128)}, bf16[4,1024,2,64]{1,3,2,0:T(8,128)(2,1)}, f32[4,2,1024]{2,1,0:T(2,128)S(1)}, bf16[4,1024,2,64]{1,3,2,0:T(8,128)(2,1)}, s32[4,1024]{...) while((s32[]{:T(128)}, ...), condition=%wide.region_3.4_spmd, body=%wide.region_0.3_spmd.sunk | while | flops 563214336 | bytes 30488668 | solution.py:134
  167.1 4.7 all-to-all-start
  182.8 15.1 %all-to-all-done = bf16[4,1024,128]{1,2,0:T(8,128)(2,1)} async-done(((bf16[4,1024,128]{1,2,0:T(8,128)(2,1)}), bf16[4,1024,128]{1,2,0:T(8,128)(2,1)}, u32[]{:S(2)}, u32[]{:S(2)}) %all-to-all-start) | async-done | bytes 1048608 | tf_op jit(solution)/shard_map/all_to_all | solution.py:138
  200.9 23.6 %multiply_convert_fusion.1 = (bf16[1024,2048]{1,0:T(8,128)(2,1)S(1)}, f32[1024,2048]{1,0:T(8,128)}, f32[1024,2048]{1,0:T(8,128)}) fusion(f32[2048]{0:T(1024)S(1)} %copy-done.19, bf16[512,2048]{1,0:T(8,128)(2,1)S(1)} %copy-done, f32[1024,512]{0,1:T(8,128)S(1)} %get-tuple-element.248, f32[512]{0:T(512)S(1)} %copy-done.21, f32[512]{0:T(512)S(1)} %copy-done.17, ...), kind=kOutput, calls=%fused_computation.68 | convolution fusion | flops 2288517120 | bytes 25186304 | tf_op jit(solution)/shard_map/dot_general | solution.py:144
  233.1 9.1 %convert_reduce_fusion = (f32[2048]{0:T(1024)S(1)}, bf16[1024,2048]{1,0:T(8,128)(2,1)S(1)}) fusion(f32[1024,2048]{1,0:T(8,128)} %get-tuple-element.246, bf16[1024,512]{0,1:T(8,128)(2,1)S(1)} %get-tuple-element.236, bf16[2048,512]{1,0:T(8,128)(2,1)S(1)} %copy-done.18, f32[1024,2048]{1,0:T(8,128)} %get-tuple-element.261, f32[2048]{0:T(1024)S(1)} %copy-done.19), kind=kOutput, calls=%fused_computation.66 | convolution fusion | flops 2183133184 | bytes 24133632 | tf_op jit(solution)/shard_map/td,fd->tf/dot_general | solution.py:155
  253.3 25.3 %all-to-all-done.1 = bf16[1024,4,128]{0,2,1:T(8,128)(2,1)} async-done(((bf16[1024,4,128]{0,2,1:T(8,128)(2,1)}), bf16[1024,4,128]{0,2,1:T(8,128)(2,1)}, u32[]{:S(2)}, u32[]{:S(2)}) %all-to-all-start.1) | async-done | bytes 1048608 | tf_op jit(solution)/shard_map/all_to_all | solution.py:172
  278.5 62.4 %while.23 = (s32[]{:T(128)}, bf16[4,1024,3,2,64]{1,4,3,2,0:T(8,128)(2,1)}, bf16[4,1024,2,64]{1,3,2,0:T(8,128)(2,1)S(1)}, s32[4,1024]{1,0:T(4,128)S(1)}, bf16[4,1...) while((s32[]{:T(128)}, ...), condition=%wide.region_14.15_spmd, body=%wide.region_12.14_spmd.sunk | while | flops 1377695744 | bytes 71375984 | solution.py:175
  340.9 6.0 copy.101
  346.9 5.1 reshape.287
  352.0 4.7 fusion.67
  357.5 7.3 %fusion.80 = f32[512,2048]{1,0:T(8,128)} fusion(bf16[1024,2048]{1,0:T(8,128)(2,1)} %copy-done.23, f32[1024,512]{0,1:T(8,128)} %copy-done.3, f32[512]{0:T(512)S(1)} %copy-done.21, f32[512]{0:T(512)S(1)} %copy-done.17, f32[1024]{0:T(1024)S(1)} %fusion.78, f32[1024]{0:T(1024)S(1)} %broadcast_multiply_fusion.1), kind=kOutput, calls=%fused_computation.141 | convolution fusion | flops 2150105088 | bytes 10498048 | tf_op jit(solution)/shard_map/dot_general | solution.py:33
  369.5 4.9 all-to-all-start.2
  377.7 6.9 fusion.92
  391.5 122.3 %all-reduce = (f32[512]{0:T(512)}, f32[512]{0:T(512)}, f32[512]{0:T(512)}, f32[2048]{0:T(1024)}, f32[512]{0:T(512)}, /*index=5*/f32[512]{0:T(512)}, f32[512]{0:T(512)}) all-reduce(f32[512]{0:T(512)S(1)} %get-tuple-element.237, f32[512]{0:T(512)S(1)} %get-tuple-element.190, ...), channel_id=1, replica_groups=mesh['batch'=8,'head'=4] {'batch','head'}, use_global_device_ids=true, to_apply=%region_21.22 | all-reduce | flops 5120 | bytes 40960 | tf_op jit(solution)/shard_map/psum | solution.py:188
  514.2 13.4 %psum.85 = bf16[2,128]{1,0:T(2,128)(2,1)S(1)} all-reduce(bf16[2,128]{1,0:T(2,128)(2,1)S(1)} %pad_maximum_fusion), channel_id=1, replica_groups=mesh['batch'=8,'head'=4] {'batch'}, use_global_device_ids=true, to_apply=%region_18.19 | all-reduce | flops 256 | bytes 1024 | tf_op jit(solution)/shard_map/psum | solution.py:186
  530.2 5.3 copy.124
  538.7 4.9 bitcast_add_fusion
  545.4 134.9 %all-reduce.7.cloned.1.call-done = (f32[512,512]{1,0:T(8,128)}, f32[512,2048]{1,0:T(8,128)}, f32[2048,512]{1,0:T(8,128)}) async-done(((f32[512,512]{1,0:T(8,128)}, f32[512,2048]{1,0:T(8,128)}, f32[2048,512]{1,0:T(8,128)}), (f32[512,512]{1,0:T(8,128)}, f32[512,2048]{1,0:T(8,128)}, f32[2048,512]{1,0:T(8,128)})) %all-reduce.7.cloned.1.call-update) | async-done | bytes 9437200 | tf_op jit(solution)/shard_map/psum | solution.py:188
  682.6 4.8 copy.151
  (171 shorter events, 177.1 us)
Async XLA Ops:
  7.2 193.6 %copy-start = (bf16[512,2048]{1,0:T(8,128)(2,1)S(1)}, bf16[512,2048]{1,0:T(8,128)(2,1)}, u32[]{:S(2)}) copy-start(bf16[512,2048]{1,0:T(8,128)(2,1)} %param.29) | copy-start | bytes 6291460
  7.2 85.9 %all-gather.3.cloned.1.call-start = ((), (), s32[]{:S(2)}) async-start(), calls=%async_computation.3 | async-start | bytes 5242880 | tf_op jit(solution)/shard_map/all_gather | solution.py:124
  167.1 30.8 %all-to-all-start = ((bf16[4,1024,128]{1,2,0:T(8,128)(2,1)}), bf16[4,1024,128]{1,2,0:T(8,128)(2,1)}, u32[]{:S(2)}, u32[]{:S(2)}) async-start(bf16[4,1024,128]{1,2,0:T(8,128)(2,1)} %bitcast.21), calls=%async_computation | async-start | bytes 2097152 | tf_op jit(solution)/shard_map/all_to_all | solution.py:138
  177.0 20.9 %copy-start.15 = (f32[512]{0:T(512)S(1)}, f32[512]{0:T(512)}, u32[]{:S(2)}) copy-start(f32[512]{0:T(512)} %param.26) | copy-start | bytes 6148
  200.5 44.8 %copy-start.3 = (f32[1024,512]{0,1:T(8,128)}, f32[1024,512]{0,1:T(8,128)S(1)}, u32[]{:S(2)}) copy-start(f32[1024,512]{0,1:T(8,128)S(1)} %get-tuple-element.248) | copy-start | bytes 6291460
  200.8 23.7 %copy-start.8 = (f32[1024,512]{0,1:T(8,128)S(1)}, f32[1024,512]{0,1:T(8,128)}, u32[]{:S(2)}) copy-start(f32[1024,512]{0,1:T(8,128)} %copy.93) | copy-start | bytes 6291460
  200.9 23.7 %copy-start.18 = (bf16[2048,512]{1,0:T(8,128)(2,1)S(1)}, bf16[2048,512]{1,0:T(8,128)(2,1)}, u32[]{:S(2)}) copy-start(bf16[2048,512]{1,0:T(8,128)(2,1)} %param.31) | copy-start | bytes 6291460
  200.9 23.7 %copy-start.20 = (f32[512]{0:T(512)S(1)}, f32[512]{0:T(512)}, u32[]{:S(2)}) copy-start(f32[512]{0:T(512)} %param.32) | copy-start | bytes 6148
  224.5 4.3 copy-start.22
  224.5 4.6 copy-start.2
  224.6 4.6 copy-start.12
  233.1 9.1 %copy-start.9 = (bf16[1024,512]{0,1:T(8,128)(2,1)}, bf16[1024,512]{0,1:T(8,128)(2,1)S(1)}, u32[]{:S(2)}) copy-start(bf16[1024,512]{0,1:T(8,128)(2,1)S(1)} %get-tuple-element.236) | copy-start | bytes 3145732
  242.3 3.0 copy-start.23
  245.9 32.6 %copy-start.5 = (bf16[4,1024,2,64]{1,3,2,0:T(8,128)(2,1)S(1)}, bf16[4,1024,2,64]{1,3,2,0:T(8,128)(2,1)}, u32[]{:S(2)}) copy-start(bf16[4,1024,2,64]{1,3,2,0:T(8,128)(2,1)} %get-tuple-element.443) | copy-start | bytes 3145732
  247.2 31.4 %copy-start.10 = (bf16[1024,512]{0,1:T(8,128)(2,1)}, bf16[1024,512]{0,1:T(8,128)(2,1)S(1)}, u32[]{:S(2)}) copy-start(bf16[1024,512]{0,1:T(8,128)(2,1)S(1)} %get-tuple-element.238) | copy-start | bytes 3145732
  249.0 29.6 %all-to-all-start.1 = ((bf16[1024,4,128]{0,2,1:T(8,128)(2,1)}), bf16[1024,4,128]{0,2,1:T(8,128)(2,1)}, u32[]{:S(2)}, u32[]{:S(2)}) async-start(bf16[1024,4,128]{0,2,1:T(8,128)(2,1)} %bitcast.24), calls=%async_computation.1 | async-start | bytes 2097152 | tf_op jit(solution)/shard_map/all_to_all | solution.py:172
  253.2 274.9 %all-reduce.5.cloned.1.call-start = ((), (), s32[]{:S(2)}) async-start(), calls=%async_computation.5 | async-start | bytes 786432 | tf_op jit(solution)/shard_map/psum | solution.py:185
  356.8 181.9 %all-gather.5.cloned.1.call-start = ((), (), s32[]{:S(2)}) async-start(), calls=%async_computation.4 | async-start | bytes 1966080 | tf_op jit(solution)/shard_map/all_gather | solution.py:125
  369.5 160.7 %all-to-all-start.2 = ((bf16[4096,3,128]{2,1,0:T(4,128)(2,1)}), bf16[4096,3,128]{2,1,0:T(4,128)(2,1)}, u32[]{:S(2)}, u32[]{:S(2)}) async-start(bf16[4096,3,128]{2,1,0:T(4,128)(2,1)} %copy.102), calls=%async_computation.2 | async-start | bytes 8388608 | tf_op jit(solution)/shard_map/all_to_all | solution.py:180
  374.3 306.0 %all-reduce.7.cloned.1.call-start = ((), (), s32[]{:S(2)}) async-start(), calls=%async_computation.6 | async-start | bytes 18874368 | tf_op jit(solution)/shard_map/psum | solution.py:188
  384.5 7.0 %copy-start.13 = (f32[512]{0:T(512)S(1)}, f32[512]{0:T(512)}, u32[]{:S(2)}) copy-start(f32[512]{0:T(512)} %get-tuple-element.188) | copy-start | bytes 6148
  384.6 7.0 %copy-start.14 = (f32[512]{0:T(512)S(1)}, f32[512]{0:T(512)}, u32[]{:S(2)}) copy-start(f32[512]{0:T(512)} %get-tuple-element.235) | copy-start | bytes 6148
  682.6 4.9 copy-start.7
  682.6 6.9 copy-start.1
  (7 other events, 14.8 us)
Sparse Core Ops, SparseCore 0:
  9.6 83.4 all-gather.2
  356.9 53.1 all-reduce.4
  411.7 70.9 all-gather.4
  489.2 191.0 all-reduce.6
where the time goes:
time: 706 us; the launch traced here: 696 us
  waiting for transfers between devices  260 us (37%)
  matrix products  150 us (21%)
  blocking collectives  136 us (19%)
  local copies, waits for them, and re-layouts  85.1 us (12%)
  other arithmetic  36.1 us (5%)
  between operations  15 us (2%)
  starting transfers between devices  14 us (2%)
    psum x1, waiting for transfers between devices, body(): lax.psum((outward_grad, outward_bias_grad, first_gain_grad, first_shift_g...  135 us
    psum x1, blocking collectives, body(): lax.psum((outward_grad, outward_bias_grad, first_gain_grad, first_shift_g...  122 us
    all_gather x1, waiting for transfers between devices, body(): lax.all_gather(stream, 'head', axis=0, tiled=True)  83.6 us
    unnamed x59, local copies, waits for them, and re-layouts  30.2 us
    all_to_all x1, waiting for transfers between devices, body(): lax.all_to_all(heads_grad, 'head', split_axis=1, concat_axis=0, tiled=True)  25.3 us
    dot_general x1, matrix products, body(): jnp.dot(first_low, up_weight, preferred_element_type=WIDE_TYPE) + up_bias  23.6 us
    dot_general x4, matrix products, attend_forward(): jnp.einsum('hqk,khe->qhe', attend_low, value_rows, preferred_element_type...  17.6 us
    dot_general x3, matrix products, contract_rows(): lax.dot_general(left, right, (((0,), (0,)), ((), ())), preferred_element_...  17.4 us
  transfers between devices with their start and end apart: 7, of which 4 were waited for; matrix products, arithmetic and copies ran while one was open for 8% of the time, Pallas kernels for 0%

commit v1 on v0

v1 whole, which is shorter than its diff:
```python
import math

import jax
import jax.numpy as jnp
from jax import lax
from jax.experimental import pallas as pl
from jax.experimental.pallas import tpu as pltpu
from jax.sharding import PartitionSpec as P

F32, BF = jnp.float32, jnp.bfloat16
ROWS, D, FF, PAIR, HD, SHORT = 1024, 512, 2048, 128, 64, 256
QB = 256
VMEM = 60 << 20
def dot(a, b): return lax.dot_general(a, b, (((1,), (0,)), ((), ())), preferred_element_type=F32)
def dot_nt(a, b): return lax.dot_general(a, b, (((1,), (1,)), ((), ())), preferred_element_type=F32)
def dot_tn(a, b): return lax.dot_general(a, b, (((0,), (0,)), ((), ())), preferred_element_type=F32)
def cp(n=1, **k): return pltpu.CompilerParams(dimension_semantics=("arbitrary",) * n, vmem_limit_bytes=VMEM, **k)

def fwd_kernel(flag, x, w, bias, e, o, qkv, rl, vt):
    wc = jnp.concatenate([w[0, 0], w[0, 1], w[0, 2]], axis=1)
    p = dot(x[...], wc)
    bq = bias[0, 0:1].astype(F32); bv = bias[0, 1:2].astype(F32)
    q = ((p[:, :PAIR] + bq).astype(BF).astype(F32) * (1.0 / math.sqrt(HD))).astype(BF)
    k = p[:, PAIR:2 * PAIR].astype(BF)
    v = (p[:, 2 * PAIR:] + bv)
    qkv[:, :PAIR] = q
    qkv[:, PAIR:2 * PAIR] = k
    qkv[:, 2 * PAIR:] = v.astype(BF)
    lane = lax.broadcasted_iota(jnp.int32, (1, PAIR), 1)
    vT = v.T.astype(BF)
    for h in range(2):
        vt[h, :HD] = vT[h * HD:(h + 1) * HD]
        vt[h, HD:] = jnp.ones((16, ROWS), BF)
    def block(qb, k0, kn):
        qs = slice(qb * QB, (qb + 1) * QB)
        parts, inv = [], []
        for h in range(2):
            qh = jnp.where(lane // HD == h, qkv[qs, :PAIR], jnp.zeros((), BF))
            s = dot_nt(qkv[k0:k0 + kn, PAIR:2 * PAIR], qh)
            m = jnp.max(s, axis=0, keepdims=True)
            ex = jnp.exp(s - m).astype(BF)
            e[0, h, 0:kn, qs] = ex
            ot = dot(vt[h, :, k0:k0 + kn], ex)
            r = 1.0 / ot[HD:HD + 1]
            parts.append(ot[:HD] * r)
            inv.append(jnp.broadcast_to(r, (HD, QB)))
        o[qs, :] = jnp.concatenate(parts, 0).T.astype(BF)
        rl[0, qs, :] = jnp.concatenate(inv, 0).T
    @pl.when(flag[0] == 1)
    def _():
        for qb in range(ROWS // QB): block(qb, 0, ROWS)
    @pl.when(flag[0] == 0)
    def _():
        for qb in range(ROWS // QB): block(qb, qb * QB, QB)

def attention_forward(flag, x, w, bias):
    n = w.shape[0]
    return pl.pallas_call(
        fwd_kernel, grid=(n,),
        in_specs=[pl.BlockSpec(memory_space=pltpu.SMEM),
                  pl.BlockSpec((ROWS, D), lambda i: (0, 0)),
                  pl.BlockSpec((1, 3, D, PAIR), lambda i: (i, 0, 0, 0)),
                  pl.BlockSpec((1, 2, PAIR), lambda i: (i, 0, 0))],
        out_specs=[pl.BlockSpec((1, 2, ROWS, ROWS), lambda i: (i, 0, 0, 0)),
                   pl.BlockSpec((ROWS, PAIR), lambda i: (0, i)),
                   pl.BlockSpec((ROWS, 3 * PAIR), lambda i: (0, i)),
                   pl.BlockSpec((1, ROWS, PAIR), lambda i: (i, 0, 0))],
        out_shape=[jax.ShapeDtypeStruct((n, 2, ROWS, ROWS), BF),
                   jax.ShapeDtypeStruct((ROWS, n * PAIR), BF),
                   jax.ShapeDtypeStruct((ROWS, n * 3 * PAIR), BF),
                   jax.ShapeDtypeStruct((n, ROWS, PAIR), F32)],
        scratch_shapes=[pltpu.VMEM((2, HD + 16, ROWS), BF)],
        compiler_params=cp(),
    )(flag, x, w, bias)

def bwd_kernel(flag, x, e, qkv, o, do, rl, g, wg, bg, vaug, doaug, ds, kt):
    lane = lax.broadcasted_iota(jnp.int32, (1, PAIR), 1)
    zero = jnp.zeros((), BF)
    dof = do[...].astype(F32) * rl[0]
    dob = dof.astype(BF)
    t = dof * o[...].astype(F32)
    th = t.astype(BF)
    tl = (t - th.astype(F32)).astype(BF)
    row = lax.broadcasted_iota(jnp.int32, (PAIR, PAIR), 0)
    col = lax.broadcasted_iota(jnp.int32, (PAIR, PAIR), 1)
    pick = jnp.where((row // HD != col // HD) & (col % HD < 2), 1.0, 0.0).astype(BF)
    delta = -(dot(th, pick) + dot(tl, pick))
    dh = delta.astype(BF)
    dl = (delta - dh.astype(F32)).astype(BF)
    dd = jnp.where(lane % HD == 0, dh, dl)
    v = qkv[:, 2 * PAIR:]
    one = jnp.ones((), BF)
    for h in range(2):
        own = lane // HD == h
        aug = (lane // HD != h) & (lane % HD < 2)
        vaug[h] = jnp.where(own, v, jnp.where(aug, one, zero))
        doaug[h] = jnp.where(own, dob, jnp.where(aug, dd, zero))
    kt[...] = qkv[:, PAIR:2 * PAIR].astype(F32).T.astype(BF)
    def score_grad(h, qs, k0, kn):
        dp = dot_nt(vaug[h, k0:k0 + kn], doaug[h, qs])
        return (e[0, h, 0:kn, qs].astype(F32) * dp).astype(BF)
    @pl.when(flag[0] == 1)
    def _():
        for qb in range(ROWS // QB):
            qs = slice(qb * QB, (qb + 1) * QB)
            dq = []
            for h in range(2):
                d = score_grad(h, qs, 0, ROWS)
                ds[h, :, qs] = d
                dq.append(dot(kt[h * HD:(h + 1) * HD], d))
            g[qs, :PAIR] = (jnp.concatenate(dq, 0).T * (1.0 / math.sqrt(HD))).astype(BF)
        q0 = [jnp.where(lane // HD == h, qkv[:, :PAIR], zero) for h in range(2)]
        d0 = [jnp.where(lane // HD == h, doaug[h], zero) for h in range(2)]
        for kb in range(ROWS // QB):
            ks = slice(kb * QB, (kb + 1) * QB)
            dk = dot(ds[0, ks], q0[0]) + dot(ds[1, ks], q0[1])
            dv = dot(e[0, 0, ks], d0[0]) + dot(e[0, 1, ks], d0[1])
            g[ks, PAIR:2 * PAIR] = dk.astype(BF)
            g[ks, 2 * PAIR:] = dv.astype(BF)
    @pl.when(flag[0] == 0)
    def _():
        for qb in range(ROWS // QB):
            qs = slice(qb * QB, (qb + 1) * QB)
            dq, dk, dv = [], 0.0, 0.0
            for h in range(2):
                own = lane // HD == h
                d = score_grad(h, qs, qb * QB, QB)
                dq.append(dot(kt[h * HD:(h + 1) * HD, qs], d))
                dk = dk + dot(d, jnp.where(own, qkv[qs, :PAIR], zero))
                dv = dv + dot(e[0, h, 0:QB, qs], jnp.where(own, doaug[h, qs], zero))
            g[qs, :PAIR] = (jnp.concatenate(dq, 0).T * (1.0 / math.sqrt(HD))).astype(BF)
            g[qs, PAIR:2 * PAIR] = dk.astype(BF)
            g[qs, 2 * PAIR:] = dv.astype(BF)
    gr = dot_tn(x[...], g[...])
    for c in range(3):
        wg[0, c] = gr[:, c * PAIR:(c + 1) * PAIR].astype(BF)
    bg[0, 0:1] = jnp.sum(g[:, :PAIR].astype(F32), 0, keepdims=True)
    bg[0, 1:2] = jnp.sum(g[:, 2 * PAIR:].astype(F32), 0, keepdims=True)

def attention_backward(flag, x, e, qkv, o, do, rl):
    n = e.shape[0]
    return pl.pallas_call(
        bwd_kernel, grid=(n,),
        in_specs=[pl.BlockSpec(memory_space=pltpu.SMEM),
                  pl.BlockSpec((ROWS, D), lambda i: (0, 0)),
                  pl.BlockSpec((1, 2, ROWS, ROWS), lambda i: (i, 0, 0, 0)),
                  pl.BlockSpec((ROWS, 3 * PAIR), lambda i: (0, i)),
                  pl.BlockSpec((ROWS, PAIR), lambda i: (0, i)),
                  pl.BlockSpec((ROWS, PAIR), lambda i: (0, i)),
                  pl.BlockSpec((1, ROWS, PAIR), lambda i: (i, 0, 0))],
        out_specs=[pl.BlockSpec((ROWS, 3 * PAIR), lambda i: (0, i)),
                   pl.BlockSpec((1, 3, D, PAIR), lambda i: (i, 0, 0, 0)),
                   pl.BlockSpec((1, 2, PAIR), lambda i: (i, 0, 0))],
        out_shape=[jax.ShapeDtypeStruct((ROWS, n * 3 * PAIR), BF),
                   jax.ShapeDtypeStruct((n, 3, D, PAIR), BF),
                   jax.ShapeDtypeStruct((n, 2, PAIR), F32)],
        scratch_shapes=[pltpu.VMEM((2, ROWS, PAIR), BF), pltpu.VMEM((2, ROWS, PAIR), BF),
                        pltpu.VMEM((2, ROWS, ROWS), BF), pltpu.VMEM((PAIR, ROWS), BF)],
        compiler_params=cp(),
    )(flag, x, e, qkv, o, do, rl)

TILE = 256
def gelu_parts(u):
    t = 1.0 / (1.0 + (0.3275911 * 0.7071067811865476) * jnp.abs(u))
    g = jnp.exp(u * u * -0.5)
    poly = t * (0.127414796 + t * (-0.142248368 + t * (0.7107068705 + t * (-0.7265760135 + t * 0.5307027145))))
    tail = poly * g
    cdf = jnp.where(u >= 0, 1.0 - tail, tail)
    return u * cdf, cdf + u * g * 0.3989422804014327

def norm_parts(h):
    m = jnp.mean(h, -1, keepdims=True)
    c = h - m
    v = jnp.mean(c * c, -1, keepdims=True)
    r = lax.rsqrt(v + 1e-5)
    return c * r, r
def norm_back(e, gain, z, r):
    eg = e * gain
    return r * (eg - jnp.mean(eg, -1, keepdims=True) - z * jnp.mean(eg * z, -1, keepdims=True))
def colsum(a): return jnp.sum(a, 0, keepdims=True)

def ffn_kernel(x, acc, oh, wo, bo, g1, s1, wu, bu, wd, bd, g2, s2, sc, ac,
               ns, na, fg, hg, dwo, dwu, dwd, vec, vup,
               low, hid, bgr, pgr, agr):
    i = pl.program_id(0)
    n = pl.num_programs(0)
    rs = pl.ds(pl.multiple_of(i * TILE, TILE), TILE)
    ot = oh[rs, :]
    att = dot(ot, wo[...]) + bo[...]
    z1, r1 = norm_parts(x[...].astype(F32) + att)
    first = z1 * g1[...] + s1[...]
    fl = first.astype(BF)
    low[rs, :] = fl
    u = dot(fl, wu[...]) + bu[...]
    a, ap = gelu_parts(u)
    ab = a.astype(BF)
    hid[rs, :] = ab
    br = dot(ab, wd[...]) + bd[...]
    na[...] = acc[...] + att + br
    z2, r2 = norm_parts(first + br)
    ns[...] = (z2 * g2[...] + s2[...]).astype(BF)
    e2 = sc[...]
    si = norm_back(e2, g2[...], z2, r2)
    bg = (si + ac[...]).astype(BF)
    bgr[rs, :] = bg
    pg = (dot_nt(bg, wd[...]) * ap).astype(BF)
    pgr[rs, :] = pg
    e1 = dot_nt(pg, wu[...]) + si
    fi = norm_back(e1, g1[...], z1, r1)
    fg[...] = fi
    ag = (fi + ac[...]).astype(BF)
    agr[rs, :] = ag
    hg[...] = dot_nt(ag, wo[...]).astype(BF)
    sums = [colsum(ag.astype(F32)), colsum(e1 * z1), colsum(e1), colsum(bg.astype(F32)), colsum(e2 * z2), colsum(e2)]
    @pl.when(i == 0)
    def _():
        vec[...] = jnp.zeros_like(vec)
        vup[...] = jnp.zeros_like(vup)
    for j, s in enumerate(sums): vec[j:j + 1, :] += s
    vup[0:1, :] += colsum(pg.astype(F32))
    @pl.when(i == n - 1)
    def _():
        dwd[...] = dot_tn(hid[...], bgr[...]).astype(BF)
        dwu[...] = dot_tn(low[...], pgr[...]).astype(BF)
        dwo[...] = dot_tn(oh[...], agr[...]).astype(BF)

def ffn(x, acc, oh, wo, bo, g1, s1, wu, bu, wd, bd, g2, s2, sc, ac):
    full = lambda a: pl.BlockSpec(a.shape, lambda i: (0,) * a.ndim)
    tile = pl.BlockSpec((TILE, D), lambda i: (i, 0))
    vs = [v.reshape(1, -1) for v in (bo, g1, s1, bu, bd, g2, s2)]
    bo, g1, s1, bu, bd, g2, s2 = vs
    S = jax.ShapeDtypeStruct
    outs = [S((ROWS, D), BF), S((ROWS, D), F32), S((ROWS, D), F32), S((ROWS, D), BF), S((D, D), BF), S((D, FF), BF), S((FF, D), BF), S((8, D), F32), S((8, FF), F32)]
    return pl.pallas_call(
        ffn_kernel, grid=(ROWS // TILE,),
        in_specs=[tile, tile, full(oh), full(wo), full(bo), full(g1), full(s1), full(wu), full(bu), full(wd), full(bd), full(g2), full(s2), tile, tile],
        out_specs=[tile, tile, tile, tile] + [full(s) for s in outs[4:]],
        out_shape=outs,
        scratch_shapes=[pltpu.VMEM((ROWS, D), BF), pltpu.VMEM((ROWS, FF), BF), pltpu.VMEM((ROWS, D), BF), pltpu.VMEM((ROWS, FF), BF), pltpu.VMEM((ROWS, D), BF)],
        compiler_params=cp(),
    )(x, acc, oh, wo, bo, g1, s1, wu, bu, wd, bd, g2, s2, sc, ac)

def back_stream_kernel(fg, g, w, out):
    t = fg[...]
    n = w.shape[0]
    for s in range(n):
        wc = jnp.concatenate([w[s, 0], w[s, 1], w[s, 2]], axis=1)
        t = t + dot_nt(g[:, s * 3 * PAIR:(s + 1) * 3 * PAIR], wc)
    out[...] = t
def back_stream(fg, g, w):
    T = 256
    return pl.pallas_call(
        back_stream_kernel, grid=(ROWS // T,),
        in_specs=[pl.BlockSpec((T, D), lambda i: (i, 0)), pl.BlockSpec((T, g.shape[1]), lambda i: (i, 0)),
                  pl.BlockSpec(w.shape, lambda i: (0, 0, 0, 0))],
        out_specs=pl.BlockSpec((T, D), lambda i: (i, 0)),
        out_shape=jax.ShapeDtypeStruct((ROWS, D), F32),
        compiler_params=cp(),
    )(fg, g, w)


def body(stream, accumulator, inward, inward_bias, outward, outward_bias, first_gain, first_shift, up_weight, up_bias,
         down_weight, down_bias, second_gain, second_shift, long_count, stream_cotangent, accumulator_cotangent):
    assert stream.shape == (ROWS, D)
    both = ("batch", "head")
    me = lax.axis_index("head")
    n_head, width = lax.axis_size("head"), inward.shape[2]
    pairs = D // PAIR
    flag = (me < long_count).astype(jnp.int32)
    full = lax.all_gather(inward, "head", axis=2, tiled=True)
    full_bias = lax.all_gather(inward_bias, "head", axis=1, tiled=True)
    w = full.reshape(3, D, pairs, PAIR).transpose(2, 0, 1, 3)
    b = full_bias.reshape(2, pairs, PAIR).transpose(1, 0, 2)
    e, o, qkv, rl = attention_forward(flag, stream, w, b)
    ns, na, fg, hg, dwo, dwu, dwd, vec, vup = ffn(
        stream, accumulator, o, outward, outward_bias, first_gain, first_shift, up_weight, up_bias, down_weight, down_bias,
        second_gain, second_shift, stream_cotangent, accumulator_cotangent)
    dwo, dwu, dwd, vec, vup = lax.psum((dwo, dwu, dwd, vec.astype(BF), vup.astype(BF)), both)
    g, wg, bg = attention_backward(flag, stream, e, qkv, o, hg, rl)
    sg = back_stream(fg, g, w)
    wg = wg.transpose(1, 2, 0, 3).reshape(3, D, D)
    bg = bg.astype(BF).transpose(1, 0, 2).reshape(2, D)
    wg = lax.psum(lax.psum_scatter(wg, "head", scatter_dimension=2, tiled=True), "batch").astype(F32)
    bg = lax.psum(lax.psum_scatter(bg, "head", scatter_dimension=1, tiled=True), "batch").astype(F32)
    dwo, dwu, dwd, vec, vup = (a.astype(F32) for a in (dwo, dwu, dwd, vec, vup))
    return (ns, na, sg, wg, bg, dwo, vec[0], vec[1], vec[2], dwu, vup[0], dwd, vec[3], vec[4], vec[5])


def solution(mesh):
    tokens = P(("batch", "head"), None)
    in_specs = (tokens, tokens, P(None, None, "head"), P(None, "head")) + (P(),) * 10 + (P("batch"), tokens, tokens)
    out_specs = (tokens,) * 3 + (P(None, None, "head"), P(None, "head")) + (P(),) * 10
    return jax.shard_map(body, mesh=mesh, in_specs=in_specs, out_specs=out_specs, check_vma=False)
```

time: 706 us -> 424 us (0.60); the launches traced: 696 us -> 424 us
  matrix products: 150 us -> 0 us
  Pallas kernels: 0 us -> 103 us
  local copies, waits for them, and re-layouts: 85.1 us -> 11.7 us
  blocking collectives: 136 us -> 65.1 us
  waiting for transfers between devices: 260 us -> 219 us
  other arithmetic: 36.1 us -> 10.2 us
  starting transfers between devices: 14 us -> 0.2 us
    dot_general x40 -> x0, matrix products: 150 us -> none  [the longest x1 23.6 us: body(): jnp.dot(first_low, up_weight, preferred_element_type=WIDE_TYPE) + up_bias]
    pallas_call x0 -> x4, Pallas kernels: none -> 103 us  [the longest x1 32.8 us: attention_backward(): pl.pallas_call(bwd_kernel, grid=(n,), in_specs=[pl.BlockSpec(memory_space...]
    psum x2, blocking collectives: 136 us -> 52.1 us  [the longest x1 40.3 us: body(): lax.psum((dwo, dwu, dwd, vec.astype(BF), vup.astype(BF)), both)]
    all_gather x2 -> x1, waiting for transfers between devices: 83.6 us -> 27.2 us  [body(): full = lax.all_gather(inward, 'head', axis=2, tiled=True)]
    psum x2, waiting for transfers between devices: 135 us -> 185 us  [the longest x1 138 us: body(): lax.psum((dwo, dwu, dwd, vec.astype(BF), vup.astype(BF)), both)]
    all_to_all x3 -> x0, waiting for transfers between devices: 40.4 us -> none  [the longest x1 25.3 us: body(): lax.all_to_all(heads_grad, 'head', split_axis=1, concat_axis=0, tiled=True)]
    unnamed x59 -> x12, local copies, waits for them, and re-layouts: 30.2 us -> 5.89 us
    while x4 -> x0, local copies, waits for them, and re-layouts: 22.4 us -> none  [the longest x3 16.4 us: body(): lax.map(attend_forward, (query_blocks, key_blocks, value_blocks, segment))]
  transfers between devices with their start and end apart: 7 -> 5, of which waited for: 4 -> 4; matrix products, arithmetic and copies ran while one was open for 8% -> 3% of each run, Pallas kernels for 0% -> 2%
where the time goes in v1:
time: 424 us
  waiting for transfers between devices  219 us (52%)
  Pallas kernels  103 us (24%)
  blocking collectives  65.1 us (15%)
  between operations  14.5 us (3%)
  local copies, waits for them, and re-layouts  11.7 us (3%)
  other arithmetic  10.2 us (2%)
    psum x1, waiting for transfers between devices, body(): lax.psum((dwo, dwu, dwd, vec.astype(BF), vup.astype(BF)), both)  138 us
    psum x1, waiting for transfers between devices, body(): lax.psum(lax.psum_scatter(wg, 'head', scatter_dimension=2, tiled=True), '...  46.8 us
    psum x1, blocking collectives, body(): lax.psum((dwo, dwu, dwd, vec.astype(BF), vup.astype(BF)), both)  40.3 us
    pallas_call x1, Pallas kernels, attention_backward(): pl.pallas_call(bwd_kernel, grid=(n,), in_specs=[pl.BlockSpec(memory_space...  32.8 us
    pallas_call x1, Pallas kernels, attention_forward(): pl.pallas_call(fwd_kernel, grid=(n,), in_specs=[pl.BlockSpec(memory_space...  32.5 us
    pallas_call x1, Pallas kernels, ffn(): pl.pallas_call(ffn_kernel, grid=(ROWS // TILE,), in_specs=[tile, tile, fu...  31.7 us
    all_gather x1, waiting for transfers between devices, body(): full = lax.all_gather(inward, 'head', axis=2, tiled=True)  27.2 us
    all_gather x1, blocking collectives, body(): full_bias = lax.all_gather(inward_bias, 'head', axis=1, tiled=True)  12.9 us
  transfers between devices with their start and end apart: 5, of which 4 were waited for; matrix products, arithmetic and copies ran while one was open for 3% of the time, Pallas kernels for 2%

profile of v1, /device:TPU:0, one launch (start us, length us, event | category | flops | bytes accessed | tf_op | source)
XLA Modules:
  0.0 423.7 jit_solution(13878022777195010686)
XLA Ops:
  7.2 1.9 copy.36
  9.9 12.9 %all_gather.7 = bf16[2,512]{1,0:T(2,128)(2,1)} all-gather(bf16[2,128]{1,0:T(2,128)(2,1)} %param.20), channel_id=1, replica_groups=mesh['batch'=8,'head'=4] {'head'}, dimensions={1}, use_global_device_ids=true | all-gather | bytes 2560 | tf_op jit(solution)/shard_map/all_gather | solution.py:271
  22.8 27.2 %all-gather.2.cloned.1.call-done = bf16[3,512,512]{1,2,0:T(8,128)(2,1)} async-done(((bf16[3,512,128]{1,2,0:T(8,128)(2,1)}), bf16[3,512,512]{1,2,0:T(8,128)(2,1)}) %all-gather.2.cloned.1.call-update) | async-done | bytes 1572880 | tf_op jit(solution)/shard_map/all_gather | solution.py:270
  50.0 2.6 copy.37
  52.6 32.5 %shard_map.280 = (bf16[4,2,1024,1024]{3,2,1,0:T(8,128)(2,1)}, bf16[1024,512]{1,0:T(8,128)(2,1)}, bf16[1024,1536]{1,0:T(8,128)(2,1)}, f32[4,1024,128]{2,1,0:T(8,128)}) custom-call(s32[1]{0:T(128)S(6)} %convert_element_type.31.flag, bf16[1024,512]{1,0:T(8,128)(2,1)} %x.5, bf16[4,3,512,128]{3,2,1,0:T(8,128)(2,1)} %bitcast.28, bf16[4,2,128]{2,1,0:T(2,128)(2,1)} %bitcast.36), custom_call_target="tpu_custom_call" | custom-call | tf_op jit(solution)/shard_map/pallas_call | solution.py:58
  85.0 31.7 %shard_map.281 = (bf16[1024,512]{1,0:T(8,128)(2,1)}, f32[1024,512]{1,0:T(8,128)}, f32[1024,512]{1,0:T(8,128)}, bf16[1024,512]{1,0:T(8,128)(2,1)}, bf16[512,512]{...) custom-call(bf16[1024,512]{1,0:T(8,128)(2,1)} %x.5, ...), custom_call_target="tpu_custom_call" | custom-call | tf_op jit(solution)/shard_map/pallas_call | solution.py:234
  116.7 32.8 %shard_map.282 = (bf16[1024,1536]{1,0:T(8,128)(2,1)}, bf16[4,3,512,128]{3,2,1,0:T(8,128)(2,1)}, f32[4,2,128]{2,1,0:T(2,128)}) custom-call(s32[1]{0:T(128)S(6)} %convert_element_type.31.flag, bf16[1024,512]{1,0:T(8,128)(2,1)} %x.5, bf16[4,2,1024,1024]{3,2,1,0:T(8,128)(2,1)} %get-tuple-element.35.e, bf16[1024,1536]{1,0:T(8,128)(2,1)} %get-tuple-element.36.qkv, ...), custom_call_target="tpu_custom_call" | custom-call | tf_op jit(solution)/shard_map/pallas_call | solution.py:142
  149.5 2.6 copy.38
  152.2 0.8 copy.40
  153.1 0.5 all-reduce.7.cloned.1.call-update
  153.9 6.5 %shard_map.283 = f32[1024,512]{1,0:T(8,128)} custom-call(f32[1024,512]{1,0:T(8,128)} %get-tuple-element.34.fg, bf16[1024,1536]{1,0:T(8,128)(2,1)} %get-tuple-element.39.g, bf16[4,3,512,128]{3,2,1,0:T(8,128)(2,1)} %bitcast.29), custom_call_target="tpu_custom_call" | custom-call | tf_op jit(solution)/shard_map/pallas_call | solution.py:252
  160.4 40.3 %all-reduce = (bf16[8,512]{1,0:T(8,128)(2,1)S(1)}, bf16[8,2048]{1,0:T(8,128)(2,1)S(1)}) all-reduce(bf16[8,512]{1,0:T(8,128)(2,1)S(1)} %convert_element_type.36, bf16[8,2048]{1,0:T(8,128)(2,1)S(1)} %convert_element_type.39), channel_id=1, replica_groups=mesh['batch'=8,'head'=4] {'batch','head'}, use_global_device_ids=true, to_apply=%region_5.0 | all-reduce | flops 20480 | bytes 81920 | tf_op jit(solution)/shard_map/psum | solution.py:278
  200.7 0.6 slice_convert_fusion
  201.3 0.6 fusion
  202.0 5.8 %reduce-scatter.7.cloned.1.call-done = bf16[128,2]{1,0:T(8,128)(2,1)} async-done(((bf16[512,2]{1,0:T(8,128)(2,1)}), bf16[128,2]{1,0:T(8,128)(2,1)}) %reduce-scatter.7.cloned.1.call-update) | async-done | bytes 528
  207.8 0.8 copy.41
  208.6 11.8 %psum.50 = bf16[2,128]{1,0:T(2,128)(2,1)S(1)} all-reduce(bf16[2,128]{1,0:T(2,128)(2,1)S(1)} %copy.41), channel_id=1, replica_groups=mesh['batch'=8,'head'=4] {'batch'}, use_global_device_ids=true, to_apply=%region_3.0 | all-reduce | flops 256 | bytes 1024 | tf_op jit(solution)/shard_map/psum | solution.py:284
  220.4 0.6 convert_element_type.34
  221.0 138.2 %all-reduce.7.cloned.1.call-done = (bf16[512,512]{1,0:T(8,128)(2,1)}, bf16[512,2048]{1,0:T(8,128)(2,1)}, bf16[2048,512]{1,0:T(8,128)(2,1)}) async-done(((bf16[512,512]{1,0:T(8,128)(2,1)}, bf16[512,2048]{1,0:T(8,128)(2,1)}, bf16[2048,512]{1,0:T(8,128)(2,1)}), (bf16[512,512]{1,0:T(8,128)(2,1)}, bf16[512,2048]{1,0:T(8,128)(2,1)}, bf16[2048,512]{1,0:T(8,128)(2,1)})) %all-reduce.7.cloned.1.call-update) | async-done | bytes 4718608 | tf_op jit(solution)/shard_map/psum | solution.py:278
  359.2 2.1 convert_element_type.35
  361.4 4.3 %convert_element_type.38 = f32[512,2048]{1,0:T(8,128)} convert(bf16[512,2048]{1,0:T(8,128)(2,1)} %get-tuple-element.80) | non-fusion elementwise | flops 1048576 | bytes 6291456 | tf_op jit(solution)/shard_map/convert_element_type | solution.py:285
  365.6 2.6 convert_element_type.40
  368.2 46.8 %all-reduce.5.cloned.1.call-done = bf16[3,512,128]{1,2,0:T(8,128)(2,1)} async-done(((bf16[3,512,128]{1,2,0:T(8,128)(2,1)}), bf16[3,512,128]{1,2,0:T(8,128)(2,1)}) %all-reduce.5.cloned.1.call-update) | async-done | bytes 393232 | tf_op jit(solution)/shard_map/psum | solution.py:283
  415.1 2.0 copy.39
  (21 shorter events, 0.6 us)
Async XLA Ops:
  7.2 42.8 %all-gather.2.cloned.1.call-start = ((), (), s32[]{:S(2)}) async-start(), calls=%async_computation.2 | async-start | bytes 1966080 | tf_op jit(solution)/shard_map/all_gather | solution.py:270
  9.2 192.2 %reduce-scatter.5.cloned.1.call-start = ((), (), s32[]{:S(2)}) async-start(), calls=%async_computation.3 | async-start | bytes 1966080 | tf_op jit(solution)/shard_map/reduce_scatter | solution.py:283
  149.5 2.7 copy-start.3
  152.1 55.6 %reduce-scatter.7.cloned.1.call-start = ((), (), s32[]{:S(2)}) async-start(), calls=%async_computation.5 | async-start | bytes 163840
  153.0 206.2 %all-reduce.7.cloned.1.call-start = ((), (), s32[]{:S(2)}) async-start(), calls=%async_computation.6 | async-start | bytes 9437184 | tf_op jit(solution)/shard_map/psum | solution.py:278
  153.1 0.7 copy-start.2
  153.1 0.8 copy-start.1
  153.6 261.5 %all-reduce.5.cloned.1.call-start = ((), (), s32[]{:S(2)}) async-start(), calls=%async_computation.4 | async-start | bytes 786432 | tf_op jit(solution)/shard_map/psum | solution.py:283
  361.4 4.3 %copy-start = (bf16[2048,512]{1,0:T(8,128)(2,1)S(1)}, bf16[2048,512]{1,0:T(8,128)(2,1)}, u32[]{:S(2)}) copy-start(bf16[2048,512]{1,0:T(8,128)(2,1)} %get-tuple-element.81) | copy-start | bytes 6291460
Sparse Core Ops, SparseCore 0:
  10.2 39.7 all-gather.1
  152.2 34.4 reduce-scatter.4
  189.5 18.1 reduce-scatter.6
  215.2 143.9 all-reduce.6
  362.1 52.9 all-reduce.4
